TPU v7x, 32 devices: a whole 2x2x4 slice. The times are simulated.
32 devices in a mesh: dp: 4 (over z), own: 8 (over y, x, core).
Axes of the slice: x: 2, y: 2, z: 4, core: 2. Of those that a mesh axis runs over, the one named last changes fastest.
Arguments:
- inputs: bfloat16 [1024, 8192], P('dp', 'own'), may hold values from -6 to 6
- out_grad: bfloat16 [1024, 8192], P('dp', 'own'), may hold values from -6 to 6
- int_values: bfloat16 [3, 3328, 128, 128], P(None, 'own'), may hold values from -127 to 127, as said below
- scales: float32 [3, 3328], P(None, 'own'), may hold values from 0.00011792096 to 0.0004684968
- block_rows: int32 [3, 128, 26], replicated, may hold values from 0 to 63, as said below
- holder: int32 [3, 128, 26], replicated, may hold values from 0 to 7, as said below
- slot_index: int32 [3, 128, 26], replicated, may hold values from 0 to 415, as said below
Outputs:
- input_grad: bfloat16 [1024, 8192], P('dp', 'own')
- grad_weights: bfloat16 [3, 3328, 128, 128], P(None, 'own', 'dp')
Inputs may be any that keep to these rules, and one draw needn't show every extreme that they name: int_values holds whole numbers. `block_rows`: the 26 row blocks of each block column of each matrix are distinct and increasing. For each matrix and each group of 16 consecutive block columns, no holder holds more than 70 of the group's blocks, and some holder holds exactly 70; each holder holds exactly 416 blocks of each matrix. For each matrix the pairs (holder, slot_index) are distinct, so every slot of every holder holds one block.
All inputs are finite; a program needn't handle non-finite values.
Results may differ from a plain program's by a relative error of at most 0.015.
Values may be sent and summed in bfloat16 or wider, within the bound.
No kernel may reach another device: no remote copies, remote signals or barrier semaphores. Data moves between devices by JAX's collectives and lax.ppermute only.
A program may use at most 512 MiB of HBM per device.

v0:
```python
import functools
import math

import jax
import jax.numpy as jnp
from jax import lax
from jax.experimental import pallas as pl
from jax.experimental.pallas import tpu as pltpu
from jax.sharding import PartitionSpec as P

F32 = jnp.float32
BF16 = jnp.bfloat16
NT = (((1,), (1,)), ((), ()))
COST = pl.CostEstimate(flops=1024, bytes_accessed=1024, transcendentals=0)
PARAMS = pltpu.CompilerParams(vmem_limit_bytes=56 * 2**20)


def whole(shape):
    return pl.BlockSpec(shape, lambda *_: (0,) * len(shape))


def waiting(after):
    return [pl.BlockSpec(memory_space=pl.ANY)] * len(after)


def mark(value):
    return value.reshape((-1,) + value.shape[-2:])[0, :16, :128]


def tie(value, *after):
    def kernel(*refs):
        pass

    return pl.pallas_call(
        kernel,
        out_shape=jax.ShapeDtypeStruct(value.shape, value.dtype),
        in_specs=waiting((value,) + after),
        out_specs=pl.BlockSpec(memory_space=pl.ANY),
        input_output_aliases={0: 0},
        compiler_params=PARAMS,
        name="tie",
    )(value, *after)


def pack(which, ints, scales, slots, quarter, rows_each, after=()):
    slot_count, block = ints.shape[1], ints.shape[2]
    places = slots.shape[0]

    def kernel(slots, quarter, scales, ints, *refs):
        out = refs[-1]

        def place(index, _):
            slot = slots[index]
            out[index] = (ints[0, slot].astype(F32) * scales[slot]).astype(BF16)
            return _

        lax.fori_loop(0, places, place, 0, unroll=8)

    return pl.pallas_call(
        kernel,
        out_shape=jax.ShapeDtypeStruct((places, rows_each, block), BF16),
        grid_spec=pltpu.PrefetchScalarGridSpec(
            num_scalar_prefetch=3,
            grid=(1,),
            in_specs=[
                pl.BlockSpec(
                    (1, slot_count, rows_each, block), lambda g, s, q, c: (which, 0, q[0], 0)
                )
            ]
            + waiting(after),
            out_specs=whole((places, rows_each, block)),
        ),
        compiler_params=PARAMS,
        cost_estimate=COST,
        name="pack",
    )(slots, quarter, scales, ints, *after)


def forward(x, arrived, flat, rows, columns, row_blocks, after=()):
    places, rows_each, block = arrived.shape
    tokens, depth = x.shape
    keep = flat.shape[0] // columns
    quarters = block // rows_each

    def kernel(flat, rows, x, arrived, *refs):
        dense, out = refs[-2:]
        step = pl.program_id(0)
        dense[...] = jnp.zeros_like(dense)
        for half in range(2):
            base = (step * 2 + half) * keep
            lanes = slice(half * block, (half + 1) * block)

            def place(k, _):
                dense[rows[base + k], :, lanes] = arrived[flat[base + k]]
                return _

            lax.fori_loop(0, keep, place, 0, unroll=13 if keep % 13 == 0 else 2)
        weights = dense[...].reshape(depth, 2 * block)
        result = jnp.dot(x[...], weights, preferred_element_type=F32)
        turned = jnp.transpose(result.astype(BF16))
        for half in range(2):
            for q in range(quarters):
                first = half * block + q * rows_each
                out[q, half] = turned[first : first + rows_each]

    return pl.pallas_call(
        kernel,
        out_shape=(
            jax.ShapeDtypeStruct((row_blocks, rows_each, columns * block), BF16),
            jax.ShapeDtypeStruct((quarters, columns, rows_each, tokens), BF16),
        ),
        grid_spec=pltpu.PrefetchScalarGridSpec(
            num_scalar_prefetch=2,
            grid=(columns // 2,),
            in_specs=[whole((tokens, depth)), whole((places, rows_each, block))] + waiting(after),
            out_specs=(
                pl.BlockSpec((row_blocks, rows_each, 2 * block), lambda g, f, r: (0, 0, g)),
                pl.BlockSpec((quarters, 2, rows_each, tokens), lambda g, f, r: (0, g, 0, 0)),
            ),
        ),
        compiler_params=PARAMS,
        cost_estimate=COST,
        name="forward",
    )(flat, rows, x, arrived, *after)


def share_specs(cotangents):
    near, early, late = cotangents
    _, tokens, width = near.shape
    others, _, first, _ = early.shape
    return [
        pl.BlockSpec((1, tokens, width), lambda g, *_: (g, 0, 0)),
        pl.BlockSpec((others, 1, first, width), lambda g, *_: (0, g, 0, 0)),
        pl.BlockSpec((1, others, tokens - first, width), lambda g, *_: (g, 0, 0, 0)),
    ]


def join(joined, quarter, near, early, late):
    planes, _, width = joined.shape
    first = early.shape[2]
    joined[quarter] = near[0]
    for shift in range(1, planes):
        plane = lax.rem(quarter + planes - shift, planes)
        joined[plane, :first] = early[shift - 1, 0]
        joined[plane, first:] = late[0, shift - 1]
    return joined[...].reshape(-1, width)


def forward_down(cotangents, arrived, flat, rows, quarter, order, columns, row_blocks):
    chips, tokens, width = cotangents[0][0].shape
    planes = cotangents[0][1].shape[0] + 1
    owners = 2 * chips
    places, rows_each, block = arrived.shape
    keep = flat.shape[0] // columns
    hidden = columns * rows_each
    per_owner = row_blocks // owners

    def kernel(flat, rows, quarter, order, *refs):
        shares, (arrived, out, joined, dense) = (refs[:3], refs[3:6]), refs[6:]
        step = pl.program_id(0)

        @pl.when(step == 0)
        def _():
            dense[...] = jnp.zeros_like(dense)
            out[...] = jnp.zeros_like(out)
            for c in range(columns):

                def place(k, _):
                    row = rows[c * keep + k]
                    lane = pl.multiple_of((row % per_owner) * block, block)
                    dense[row // per_owner, c * rows_each : (c + 1) * rows_each, pl.ds(lane, block)] = (
                        arrived[flat[c * keep + k]]
                    )
                    return _

                lax.fori_loop(0, keep, place, 0, unroll=13 if keep % 13 == 0 else 2)

        for core in range(2):
            out[...] += lax.dot_general(
                dense[order[2 * step + core]],
                join(joined, quarter[0], *shares[core]),
                NT,
                preferred_element_type=F32,
            )

    share = share_specs(cotangents[0])
    return pl.pallas_call(
        kernel,
        out_shape=jax.ShapeDtypeStruct((hidden, planes * tokens), F32),
        grid_spec=pltpu.PrefetchScalarGridSpec(
            num_scalar_prefetch=4,
            grid=(chips,),
            in_specs=share + share + [whole((places, rows_each, block))],
            out_specs=whole((hidden, planes * tokens)),
            scratch_shapes=[
                pltpu.VMEM((planes, tokens, width), BF16),
                pltpu.VMEM((owners, hidden, width), BF16),
            ],
        ),
        compiler_params=PARAMS,
        cost_estimate=COST,
        name="forward_down",
    )(flat, rows, quarter, order, *cotangents[0], *cotangents[1], arrived)


def weight_grad(x_turned, grad, flat, rows, places, row_blocks, factor, after=()):
    quarters, columns, rows_each, tokens = grad.shape
    depth = x_turned.shape[0]
    block = quarters * rows_each
    keep = flat.shape[0] // columns

    def kernel(flat, rows, x_turned, grad, *refs):
        out, result = refs[-2:]
        step = pl.program_id(0)
        right = jnp.concatenate(
            [grad[q, half] for half in range(2) for q in range(quarters)], axis=0
        )
        product = lax.dot_general(x_turned[...], right, NT, preferred_element_type=F32)
        result[...] = (product * factor).astype(BF16).reshape(result.shape)
        for half in range(2):
            base = (step * 2 + half) * keep
            lanes = slice(half * block, (half + 1) * block)

            def place(k, _):
                out[flat[base + k]] = result[rows[base + k], :, lanes]
                return _

            lax.fori_loop(0, keep, place, 0, unroll=13 if keep % 13 == 0 else 2)

    return pl.pallas_call(
        kernel,
        out_shape=jax.ShapeDtypeStruct((places, rows_each, block), BF16),
        grid_spec=pltpu.PrefetchScalarGridSpec(
            num_scalar_prefetch=2,
            grid=(columns // 2,),
            in_specs=[
                whole((depth, tokens)),
                pl.BlockSpec((quarters, 2, rows_each, tokens), lambda g, f, r: (0, g, 0, 0)),
            ]
            + waiting(after),
            out_specs=whole((places, rows_each, block)),
            scratch_shapes=[pltpu.VMEM((row_blocks, rows_each, 2 * block), BF16)],
        ),
        compiler_params=PARAMS,
        cost_estimate=COST,
        name="weight_grad",
    )(flat, rows, x_turned, grad, *after)


def weight_grad_down(
    value, cotangents, flat, rows, quarter, order, places, block, columns, row_blocks, factor
):
    chips, tokens, width = cotangents[0][0].shape
    planes = cotangents[0][1].shape[0] + 1
    owners = 2 * chips
    hidden = value.shape[0]
    rows_each = hidden // columns
    keep = flat.shape[0] // columns
    per_owner = row_blocks // owners

    def kernel(flat, rows, quarter, order, value, *refs):
        shares, (out, joined, result) = (refs[:3], refs[3:6]), refs[6:]
        step = pl.program_id(0)
        for core in range(2):
            right = join(joined, quarter[0], *shares[core])
            product = jnp.dot(value[...], right, preferred_element_type=F32)
            result[order[2 * step + core]] = (product * factor).astype(BF16)

        @pl.when(step == chips - 1)
        def _():
            for c in range(columns):

                def place(k, _):
                    row = rows[c * keep + k]
                    lane = pl.multiple_of((row % per_owner) * block, block)
                    out[flat[c * keep + k]] = result[
                        row // per_owner, c * rows_each : (c + 1) * rows_each, pl.ds(lane, block)
                    ]
                    return _

                lax.fori_loop(0, keep, place, 0, unroll=13 if keep % 13 == 0 else 2)

    share = share_specs(cotangents[0])
    return pl.pallas_call(
        kernel,
        out_shape=jax.ShapeDtypeStruct((places, rows_each, block), BF16),
        grid_spec=pltpu.PrefetchScalarGridSpec(
            num_scalar_prefetch=4,
            grid=(chips,),
            in_specs=[whole((hidden, planes * tokens))] + share + share,
            out_specs=whole((places, rows_each, block)),
            scratch_shapes=[
                pltpu.VMEM((planes, tokens, width), BF16),
                pltpu.VMEM((owners, hidden, width), BF16),
            ],
        ),
        compiler_params=PARAMS,
        cost_estimate=COST,
        name="weight_grad_down",
    )(flat, rows, quarter, order, value, *cotangents[0], *cotangents[1])


def input_part(weights, grad, first, chips, earlier=(), after=()):
    depth, units = weights.shape
    quarters, columns, rows_each, tokens = grad.shape
    rows = depth // (2 * chips)

    def kernel(first, left, right, grad, *refs):
        earlier, (*outs, natural) = refs[: len(refs) - len(after) - 3], refs[-3:]

        @pl.when(pl.program_id(0) == 0)
        def _():
            for c in range(columns):
                for q in range(quarters):
                    natural[c, q] = grad[q, c]

        both = jnp.concatenate([left[...], right[...]], axis=0)
        product = jnp.dot(
            both, natural[...].reshape(units, tokens), preferred_element_type=F32
        )
        for core in range(2):
            part = product[core * rows : (core + 1) * rows]
            if earlier:
                part = earlier[core][0] + part
            outs[core][0] = part.astype(outs[core].dtype)

    share = pl.BlockSpec((1, rows, tokens), lambda g, f: (g, 0, 0))
    out = jax.ShapeDtypeStruct((chips, rows, tokens), BF16 if earlier else F32)
    return pl.pallas_call(
        kernel,
        out_shape=(out, out),
        grid_spec=pltpu.PrefetchScalarGridSpec(
            num_scalar_prefetch=1,
            grid=(chips,),
            in_specs=[
                pl.BlockSpec((rows, units), lambda g, f: (2 * g + f[0], 0)),
                pl.BlockSpec((rows, units), lambda g, f: (2 * g + 1 - f[0], 0)),
                whole(grad.shape),
            ]
            + [share] * len(earlier)
            + waiting(after),
            out_specs=(share, share),
            scratch_shapes=[pltpu.VMEM((columns, quarters, rows_each, tokens), BF16)],
        ),
        compiler_params=PARAMS,
        cost_estimate=COST,
        name="input_part",
    )(first, weights, weights, grad, *earlier, *after)


def unpack(which, returned, source, total):
    places, rows_each, block = returned.shape
    slot_count = source.shape[0]

    def kernel(source, returned, *refs):
        out = refs[-1]

        def place(slot, _):
            out[0, slot] = returned[source[slot]]
            return _

        lax.fori_loop(0, slot_count, place, 0, unroll=8)

    shape = (3, slot_count, rows_each, block)
    extra = [] if total is None else [total]
    return pl.pallas_call(
        kernel,
        out_shape=jax.ShapeDtypeStruct(shape, BF16),
        grid_spec=pltpu.PrefetchScalarGridSpec(
            num_scalar_prefetch=1,
            grid=(1,),
            in_specs=[whole((places, rows_each, block))] + waiting(extra),
            out_specs=pl.BlockSpec((1,) + shape[1:], lambda g, s: (which, 0, 0, 0)),
        ),
        input_output_aliases={2: 0} if extra else {},
        compiler_params=PARAMS,
        cost_estimate=COST,
        name="unpack",
    )(source, returned, *extra)


def in_order(kept, quarter, after=()):
    count, shape = len(kept), kept[0].shape

    def kernel(quarter, *refs):
        for shift in range(count):
            refs[-1][lax.rem(quarter[0] + count - shift, count)] = refs[shift][...]

    return pl.pallas_call(
        kernel,
        out_shape=jax.ShapeDtypeStruct((count,) + shape, kept[0].dtype),
        grid_spec=pltpu.PrefetchScalarGridSpec(
            num_scalar_prefetch=1,
            grid=(1,),
            in_specs=[whole(shape)] * count + waiting(after),
            out_specs=whole((count,) + shape),
        ),
        compiler_params=PARAMS,
        cost_estimate=COST,
        name="in_order",
    )(quarter, *kept, *after)


def silu_parts(gate, up_value, grad_act):
    sigmoid_g = jax.nn.sigmoid(gate)
    activated = gate * sigmoid_g
    value = (activated * up_value).astype(BF16)
    grad_gate = (grad_act * up_value * sigmoid_g * (1.0 + gate * (1.0 - sigmoid_g))).astype(BF16)
    grad_up = (grad_act * activated).astype(BF16)
    return (value, grad_gate, grad_up)


def per_device(inputs, out_grad, int_values, scales, block_rows, holder, slot_index):
    own_count = lax.axis_size("own")
    data_count = lax.axis_size("dp")
    own_index = lax.axis_index("own")
    data_index = lax.axis_index("dp")
    local_tokens, local_width = inputs.shape
    tokens = local_tokens * data_count
    slot_count = int_values.shape[1]
    block = int_values.shape[2]
    keep = block_rows.shape[2]
    width = local_width * own_count
    row_blocks = width // block
    columns = block_rows.shape[1] // own_count
    group = columns * keep
    active = 3 * own_count // 4
    capacity = (group + active - 1) // active
    places = own_count * capacity
    rows_each = block // data_count
    depth = row_blocks * rows_each
    hidden = columns * rows_each
    factor = 1.0 / math.sqrt(tokens)

    holder_group = holder.reshape(3, own_count, group)
    slot_group = slot_index.reshape(3, own_count, group)
    mine = (holder_group == own_index).astype(jnp.int32)
    rank = jnp.cumsum(mine, axis=2) - 1
    spots = jnp.arange(capacity, dtype=jnp.int32)
    picked = (mine[..., None] == 1) & (rank[..., None] == spots)
    bucket_slot = jnp.sum(jnp.where(picked, slot_group[..., None], 0), axis=2)
    used = spots < jnp.sum(mine, axis=2)[..., None]
    hits = used[..., None] & (bucket_slot[..., None] == jnp.arange(slot_count, dtype=jnp.int32))
    bucket_index = jnp.arange(places, dtype=jnp.int32).reshape(own_count, capacity)
    source = jnp.sum(jnp.where(hits, bucket_index[None, :, :, None], 0), axis=(1, 2))
    bucket_slot = bucket_slot.reshape(3, places)
    own_holder = lax.dynamic_index_in_dim(holder_group, own_index, 1, keepdims=False)
    entries = jnp.arange(group, dtype=jnp.int32)
    earlier = (own_holder[:, :, None] == own_holder[:, None, :]) & (
        entries[None, :, None] < entries[None, None, :]
    )
    position = jnp.sum(earlier.astype(jnp.int32), axis=1)
    flat = own_holder * capacity + position
    rows = lax.dynamic_index_in_dim(
        block_rows.reshape(3, own_count, group), own_index, 1, keepdims=False
    )
    quarter = data_index.astype(jnp.int32).reshape(1)

    def exchange(parts):
        kept = [parts[0]]
        for s in range(1, data_count):
            turn = [(i, (i + s) % data_count) for i in range(data_count)]
            kept.append(lax.ppermute(parts[s], "dp", turn))
        return kept

    def to_planes(parts):
        twice = jnp.concatenate([parts, parts])
        return [
            lax.dynamic_index_in_dim(twice, data_index + s, 0, keepdims=False)
            for s in range(data_count)
        ]

    def send(which, after=()):
        sending = pack(
            which, int_values, scales[which], bucket_slot[which], quarter, rows_each, after
        )
        return sending.reshape(own_count, capacity, rows_each, block)

    def receive(sending):
        arrived = lax.all_to_all(sending, "own", split_axis=0, concat_axis=0, tiled=True)
        return arrived.reshape(places, rows_each, block)

    chips = own_count // 2
    likes = [[core + 2 * chip for chip in range(chips)] for core in range(2)]
    swap = [(i, i ^ 1) for i in range(own_count)]
    core = jnp.remainder(own_index, 2).astype(jnp.int32).reshape(1)
    turns = own_index ^ (2 * jnp.arange(chips, dtype=jnp.int32))
    order = jnp.stack([turns, turns ^ 1], axis=1).reshape(own_count)

    def over_chips(value):
        turns = [[(i, i ^ (2 * turn)) for i in range(own_count)] for turn in range(1, chips)]
        return [value] + [lax.ppermute(value, "own", turn) for turn in turns]

    near = over_chips(out_grad)
    gone = tuple(mark(part) for part in near[1:])
    near = jnp.stack(near)
    cut = local_tokens // 8
    bundle = jnp.concatenate([near[:, :cut].reshape(chips * cut, local_width), out_grad[cut:]])
    bundles = exchange([bundle] * data_count)[1:]

    early = [part[: chips * cut].reshape(chips, cut, local_width) for part in bundles]
    late = [part[chips * cut :] for part in bundles]

    local = inputs.reshape(local_tokens, row_blocks // own_count, data_count, rows_each)
    local = local.transpose(2, 0, 1, 3).reshape(data_count, local_tokens, depth // own_count)
    local = exchange(to_planes(local))
    sending_gate = send(0)
    local = in_order(local, quarter, (mark(sending_gate),) + gone)
    gathered = lax.all_gather(local.reshape(tokens, depth // own_count), "own", axis=0)
    sending_up, sending_down = send(1, (mark(local),)), send(2, (mark(local),))
    arrived_gate = receive(sending_gate)

    x = gathered.transpose(1, 0, 2).reshape(tokens, depth)
    x_turned = gathered.transpose(0, 2, 1).reshape(depth, tokens)
    packed = (mark(sending_up), mark(sending_down)) + tuple(mark(part) for part in bundles)
    gate_weights, part = forward(x, arrived_gate, flat[0], rows[0], columns, row_blocks, packed)
    gate = lax.psum_scatter(part, "dp", scatter_dimension=0)
    late = over_chips(tie(jnp.stack(late), mark(gate_weights)))
    arrived_up = receive(tie(sending_up, mark(gate_weights)))
    up_weights, part = forward(
        x,
        arrived_up,
        flat[1],
        rows[1],
        columns,
        row_blocks,
        (mark(gate),) + tuple(mark(part) for part in late[1:]),
    )
    up_value = lax.psum_scatter(part, "dp", scatter_dimension=0)
    cotangents = (near, jnp.stack(early), jnp.stack(late))
    cotangents = (cotangents, [lax.ppermute(part, "own", swap) for part in cotangents])
    arrived_down = receive(tie(sending_down, mark(arrived_up)))
    grad_act = forward_down(
        cotangents, arrived_down, flat[2], rows[2], quarter, order, columns, row_blocks
    )
    value, grad_gate, grad_up = silu_parts(
        gate.reshape(hidden, tokens).astype(F32), up_value.reshape(hidden, tokens).astype(F32), grad_act
    )
    shape = (columns, rows_each, tokens)

    def give_back(leaving):
        leaving = leaving.reshape(own_count, capacity, rows_each, block)
        returned = lax.all_to_all(leaving, "own", split_axis=0, concat_axis=0, tiled=True)
        return returned.reshape(places, rows_each, block)

    all_up = lax.all_gather(grad_up.reshape(shape), "dp", axis=0)
    leaving = weight_grad_down(
        value, cotangents, flat[2], rows[2], quarter, order, places, block, columns, row_blocks, factor
    )
    all_gate = lax.all_gather(grad_gate.reshape(shape), "dp", axis=0)
    returned = give_back(leaving)
    leaving = weight_grad(
        x_turned, all_up, flat[1], rows[1], places, row_blocks, factor, (mark(returned),)
    )
    total = unpack(2, returned, source[2], None)
    returned = give_back(leaving)

    up_weights = up_weights.reshape(depth, columns * block)
    gate_weights = gate_weights.reshape(depth, columns * block)
    back = input_part(up_weights, all_up, core, chips, after=(mark(leaving),))
    back = input_part(gate_weights, all_gate, core, chips, back, (mark(returned), mark(total)))
    leaving = weight_grad(
        x_turned, all_gate, flat[0], rows[0], places, row_blocks, factor, (mark(back[0]),)
    )
    total = unpack(1, returned, source[1], total)
    returned = give_back(leaving)

    back = back[0].astype(F32) + lax.ppermute(back[1], "own", swap).astype(F32)
    back = lax.psum_scatter(
        back.astype(BF16), "own", scatter_dimension=0, axis_index_groups=likes
    )
    back = back.reshape(depth // own_count, data_count, local_tokens).transpose(1, 0, 2)
    back = tie(back, mark(total))
    back = in_order(exchange(to_planes(back)), quarter)
    back = back.reshape(data_count, row_blocks // own_count, rows_each, local_tokens)
    input_grad = back.transpose(3, 1, 0, 2).reshape(local_tokens, local_width)
    total = unpack(0, returned, source[0], total)
    return (input_grad, total)


def solution(mesh):
    placed = (
        P("dp", "own"),
        P("dp", "own"),
        P(None, "own", None, None),
        P(None, "own"),
        P(),
        P(),
        P(),
    )
    return jax.shard_map(
        per_device,
        mesh=mesh,
        in_specs=placed,
        out_specs=(P("dp", "own"), P(None, "own", "dp", None)),
        check_vma=False,
    )
```

profile of v0, /device:TPU:0, one launch (start us, length us, event | category | flops | bytes accessed | tf_op | source)
XLA Modules:
  0.0 658.4 jit_solution(4570758823405419699)
XLA Ops:
  7.2 4.0 collective-permute-start.5
  13.5 2.0 collective-permute-start
  15.6 2.7 collective-permute-start.1
  18.6 3.4 reduce-window.6
  22.7 3.6 select_reduce_fusion.1
  29.0 6.2 pack.3
  35.2 1.3 slice_bitcast_fusion.22.refs_4_
  37.3 1.3 collective-permute-start.2
  40.6 1.7 collective-permute-done.2.refs_3_
  42.9 1.9 in_order.2
  44.9 4.7 all-to-all-start
  51.3 1.7 pad_maximum_fusion.1.refs_0_
  54.1 3.1 collective-permute-start.8
  57.7 1.4 constant_dynamic-slice_fusion.2
  63.9 6.1 pack.4
  70.0 6.2 pack.5
  76.3 1.3 slice_bitcast_fusion.16
  78.2 40.2 %collective-permute-done.7 = bf16[352,1024]{1,0:T(8,128)(2,1)S(1)} collective-permute-done((bf16[352,1024]{1,0:T(8,128)(2,1)}, bf16[352,1024]{1,0:T(8,128)(2,1)S(1)}, u32[]{:S(2)}, u32[]{:S(2)}) %collective-permute-start.7) | collective-permute-done | bytes 720928 | tf_op jit(solution)/shard_map/ppermute | solution.py:463
  120.5 4.8 copy.83
  125.2 17.7 %forward.2 = (bf16[64,32,2048]{2,1,0:T(8,128)(2,1)}, bf16[4,16,32,1024]{3,2,1,0:T(8,128)(2,1)}) custom-call(s32[416]{0:T(512)} %bitcast.205, s32[416]{0:T(512)} %bitcast.203, bf16[1024,2048]{1,0:T(8,128)(2,1)} %bitcast.152, bf16[560,32,128]{2,1,0:T(8,128)(2,1)} %bitcast.24.arrived, bf16[16,128]{1,0:T(8,128)(2,1)} %get-tuple-element.57.refs_0_, ...), custom_call_target="tpu_custom_call" | custom-call | flops 1024 | bytes 1024 | tf_op jit(solution)/shard_map/forward/pallas_call | solution.py:106
  144.2 4.6 all-to-all-start.1
  150.0 1.3 pad_maximum_fusion.2.refs_0_
  151.3 1.9 collective-permute-start.9
  153.2 1.5 collective-permute-start.11
  154.8 76.3 %collective-permute-done.9 = bf16[3,224,1024]{2,1,0:T(8,128)(2,1)S(1)} collective-permute-done((bf16[3,224,1024]{2,1,0:T(8,128)(2,1)}, bf16[3,224,1024]{2,1,0:T(8,128)(2,1)S(1)}, u32[]{:S(2)}, u32[]{:S(2)}) %collective-permute-start.9) | collective-permute-done | bytes 1376288 | tf_op jit(solution)/shard_map/ppermute | solution.py:492
  232.9 28.2 %collective-permute-done.11 = bf16[3,224,1024]{2,1,0:T(8,128)(2,1)S(1)} collective-permute-done((bf16[3,224,1024]{2,1,0:T(8,128)(2,1)}, bf16[3,224,1024]{2,1,0:T(8,128)(2,1)S(1)}, u32[]{:S(2)}, u32[]{:S(2)}) %collective-permute-start.11) | collective-permute-done | bytes 1376288 | tf_op jit(solution)/shard_map/ppermute | solution.py:492
  264.4 1.3 slice_bitcast_fusion.11.refs_0_
  265.7 17.7 %forward.3 = (bf16[64,32,2048]{2,1,0:T(8,128)(2,1)}, bf16[4,16,32,1024]{3,2,1,0:T(8,128)(2,1)}) custom-call(s32[416]{0:T(512)} %bitcast.209, s32[416]{0:T(512)} %bitcast.207, bf16[1024,2048]{1,0:T(8,128)(2,1)} %bitcast.153, bf16[560,32,128]{2,1,0:T(8,128)(2,1)} %bitcast.54.arrived, bf16[16,128]{1,0:T(8,128)(2,1)} %slice_bitcast_fusion.11.refs_0_, ...), custom_call_target="tpu_custom_call" | custom-call | flops 1024 | bytes 1024 | tf_op jit(solution)/shard_map/forward/pallas_call | solution.py:106
  283.5 1.3 copy-done.1
  284.8 5.3 pad_maximum_fusion.refs_2_
  290.1 1.3 slice_bitcast_fusion.12.refs_1_
  291.4 4.6 all-to-all-start.2
  300.6 3.6 collective-permute-done.13.refs_4_
  304.3 45.1 %all-to-all-done.2 = bf16[8,70,32,128]{3,2,1,0:T(8,128)(2,1)} async-done(((bf16[8,70,32,128]{3,2,1,0:T(8,128)(2,1)}), bf16[8,70,32,128]{3,2,1,0:T(8,128)(2,1)}, u32[]{:S(2)}, u32[]{:S(2)}) %all-to-all-start.2) | async-done | bytes 4587552 | tf_op jit(solution)/shard_map/all_to_all | solution.py:480
  349.4 20.7 %forward_down.1 = f32[512,1024]{1,0:T(8,128)} custom-call(s32[416]{0:T(512)} %bitcast.201, s32[416]{0:T(512)} %bitcast.199, s32[1]{0:T(128)} %bitcast.quarter, s32[8]{0:T(128)} %reshape.209.order, bf16[4,256,1024]{2,1,0:T(8,128)(2,1)} %copy-done, bf16[3,4,32,1024]{3,2,1,0:T(8,128)(2,1)} %copy-done.2, bf16[4,3,224,1024]{3,2,1,0:T(8,128)(2,1)} %pad_maximum_fusion.refs_2_, ...), custom_call_target="tpu_custom_call" | custom-call | flops 1024 | bytes 1024 | tf_op jit(solution)/shard_map/forward_down/pallas_call | solution.py:187
  370.1 5.3 multiply_convert_fusion
  375.4 19.6 %weight_grad_down.1 = bf16[560,32,128]{2,1,0:T(8,128)(2,1)} custom-call(s32[416]{0:T(512)} %bitcast.202, s32[416]{0:T(512)} %bitcast.200, s32[1]{0:T(128)} %bitcast.quarter, s32[8]{0:T(128)} %reshape.209.order, bf16[512,1024]{1,0:T(8,128)(2,1)} %get-tuple-element.30.value, bf16[4,256,1024]{2,1,0:T(8,128)(2,1)} %copy-done, ...), custom_call_target="tpu_custom_call" | custom-call | flops 1024 | bytes 1024 | tf_op jit(solution)/shard_map/weight_grad_down/pallas_call | solution.py:284
  394.9 4.6 all-to-all-start.3
  400.2 6.5 copy.77
  406.6 46.3 %all-to-all-done.3 = bf16[8,70,32,128]{3,2,1,0:T(8,128)(2,1)} async-done(((bf16[8,70,32,128]{3,2,1,0:T(8,128)(2,1)}), bf16[8,70,32,128]{3,2,1,0:T(8,128)(2,1)}, u32[]{:S(2)}, u32[]{:S(2)}) %all-to-all-start.3) | async-done | bytes 4587552 | tf_op jit(solution)/shard_map/all_to_all | solution.py:543
  452.9 1.3 slice_bitcast_fusion.7.refs_0_
  454.2 1.6 all-gather.8.cloned.1.call-done.grad
  455.8 17.2 %weight_grad.2 = bf16[560,32,128]{2,1,0:T(8,128)(2,1)} custom-call(s32[416]{0:T(512)} %bitcast.210, s32[416]{0:T(512)} %bitcast.208, bf16[2048,1024]{1,0:T(8,128)(2,1)} %bitcast.154, bf16[4,16,32,1024]{3,2,1,0:T(8,128)(2,1)} %all-gather.8.cloned.1.call-done.grad, bf16[16,128]{1,0:T(8,128)(2,1)} %slice_bitcast_fusion.7.refs_0_), custom_call_target="tpu_custom_call" | custom-call | flops 1024 | bytes 1024 | tf_op jit(solution)/shard_map/weight_grad/pallas_call | solution.py:230
  473.0 4.7 all-to-all-start.4
  479.7 5.5 unpack.3.refs_0_
  487.7 13.9 %input_part.2 = (f32[4,256,1024]{2,1,0:T(8,128)}, f32[4,256,1024]{2,1,0:T(8,128)}) custom-call(s32[1]{0:T(128)} %bitcast.1.first, bf16[2048,2048]{1,0:T(8,128)(2,1)} %bitcast.158, bf16[2048,2048]{1,0:T(8,128)(2,1)} %bitcast.159, bf16[4,16,32,1024]{3,2,1,0:T(8,128)(2,1)} %all-gather.8.cloned.1.call-done.grad, bf16[16,128]{1,0:T(8,128)(2,1)} %slice_bitcast_fusion.6.refs_0_), custom_call_target="tpu_custom_call" | custom-call | flops 1024 | bytes 1024 | tf_op jit(solution)/shard_map/input_part/pallas_call | solution.py:329
  501.7 29.4 %all-to-all-done.4 = bf16[8,70,32,128]{3,2,1,0:T(8,128)(2,1)} async-done(((bf16[8,70,32,128]{3,2,1,0:T(8,128)(2,1)}), bf16[8,70,32,128]{3,2,1,0:T(8,128)(2,1)}, u32[]{:S(2)}, u32[]{:S(2)}) %all-to-all-start.4) | async-done | bytes 4587552 | tf_op jit(solution)/shard_map/all_to_all | solution.py:543
  531.1 1.3 slice_bitcast_fusion.5.refs_2_
  532.4 4.1 all-gather.6.cloned.1.call-done.grad
  536.5 14.5 %input_part.3 = (bf16[4,256,1024]{2,1,0:T(8,128)(2,1)}, bf16[4,256,1024]{2,1,0:T(8,128)(2,1)}) custom-call(s32[1]{0:T(128)} %bitcast.1.first, bf16[2048,2048]{1,0:T(8,128)(2,1)} %bitcast.156, bf16[2048,2048]{1,0:T(8,128)(2,1)} %bitcast.157, bf16[4,16,32,1024]{3,2,1,0:T(8,128)(2,1)} %all-gather.6.cloned.1.call-done.grad, ...), custom_call_target="tpu_custom_call" | custom-call | flops 1024 | bytes 1024 | tf_op jit(solution)/shard_map/input_part/pallas_call | solution.py:329
  551.1 4.4 collective-permute-done.15
  555.5 3.9 add_convert_fusion
  560.6 17.2 %weight_grad.3 = bf16[560,32,128]{2,1,0:T(8,128)(2,1)} custom-call(s32[416]{0:T(512)} %bitcast.206, s32[416]{0:T(512)} %bitcast.204, bf16[2048,1024]{1,0:T(8,128)(2,1)} %bitcast.155, bf16[4,16,32,1024]{3,2,1,0:T(8,128)(2,1)} %all-gather.6.cloned.1.call-done.grad, bf16[16,128]{1,0:T(8,128)(2,1)} %slice_bitcast_fusion.23.refs_0_), custom_call_target="tpu_custom_call" | custom-call | flops 1024 | bytes 1024 | tf_op jit(solution)/shard_map/weight_grad/pallas_call | solution.py:230
  577.8 4.6 all-to-all-start.5
  582.4 5.8 unpack.4.refs_0_
  588.2 1.3 slice_bitcast_fusion.3.refs_1_
  589.5 9.3 %reduce-scatter.10.cloned.1.call-done = bf16[1,256,1024]{2,1,0:T(8,128)(2,1)} async-done(((bf16[4,256,1024]{2,1,0:T(8,128)(2,1)}), bf16[1,256,1024]{2,1,0:T(8,128)(2,1)}) %reduce-scatter.10.cloned.1.call-update) | async-done | bytes 524304
  601.0 1.9 fusion.21
  603.0 1.7 collective-permute-start.16
  604.7 2.4 collective-permute-start.17
  607.1 1.4 collective-permute-start.18
  608.5 32.9 %all-to-all-done.5 = bf16[8,70,32,128]{3,2,1,0:T(8,128)(2,1)} async-done(((bf16[8,70,32,128]{3,2,1,0:T(8,128)(2,1)}), bf16[8,70,32,128]{3,2,1,0:T(8,128)(2,1)}, u32[]{:S(2)}, u32[]{:S(2)}) %all-to-all-start.5) | async-done | bytes 4587552 | tf_op jit(solution)/shard_map/all_to_all | solution.py:543
  641.4 5.4 unpack.5
  647.6 1.9 in_order.3
  (168 shorter events, 43.8 us)
Async XLA Ops:
  7.2 11.1 %copy-start.16 = (s32[3,128,26]{1,2,0:T(8,128)S(1)}, s32[3,128,26]{1,2,0:T(8,128)}, u32[]{:S(2)}) copy-start(s32[3,128,26]{1,2,0:T(8,128)} %param.12) | copy-start | bytes 119812
  7.2 15.3 %copy-start.24 = (s32[3,128,26]{1,2,0:T(8,128)S(1)}, s32[3,128,26]{1,2,0:T(8,128)}, u32[]{:S(2)}) copy-start(s32[3,128,26]{1,2,0:T(8,128)} %param.13) | copy-start | bytes 119812
  7.2 20.5 %copy-start.26 = (f32[3,416]{1,0:T(4,128)S(1)}, f32[3,416]{1,0:T(4,128)}, u32[]{:S(2)}) copy-start(f32[3,416]{1,0:T(4,128)} %param.10) | copy-start | bytes 14980
  7.2 113.3 %all-gather.4.cloned.1.call-start = ((), (), s32[]{:S(2)}) async-start(), calls=%async_computation.9 | async-start | bytes 4718592 | tf_op jit(solution)/shard_map/all_gather | solution.py:509
  7.2 30.1 %collective-permute-start.5 = (bf16[256,1024]{1,0:T(8,128)(2,1)}, bf16[256,1024]{1,0:T(8,128)(2,1)S(1)}, u32[]{:S(2)}, u32[]{:S(2)}) collective-permute-start(bf16[256,1024]{1,0:T(8,128)(2,1)} %param.8), channel_id=1, source_target_pairs={{0,6},{1,7},{2,4},{3,5},{4,2},{5,3},{6,0},{7,1},{8,14},{9,15},{10,... | collective-permute-start | bytes 1572872 | tf_op jit(solution)/shard_map/ppermute | solution.py:492
  11.2 28.1 %collective-permute-start.4 = (bf16[256,1024]{1,0:T(8,128)(2,1)}, bf16[256,1024]{1,0:T(8,128)(2,1)S(1)}, u32[]{:S(2)}, u32[]{:S(2)}) collective-permute-start(bf16[256,1024]{1,0:T(8,128)(2,1)} %param.8), channel_id=1, source_target_pairs={{0,4},{1,5},{2,6},{3,7},{4,0},{5,1},{6,2},{7,3},{8,12},{9,13},{10,... | collective-permute-start | bytes 1572872 | tf_op jit(solution)/shard_map/ppermute | solution.py:492
  11.7 28.2 %collective-permute-start.3 = (bf16[256,1024]{1,0:T(8,128)(2,1)}, bf16[256,1024]{1,0:T(8,128)(2,1)S(1)}, u32[]{:S(2)}, u32[]{:S(2)}) collective-permute-start(bf16[256,1024]{1,0:T(8,128)(2,1)} %param.8), channel_id=1, source_target_pairs={{0,2},{1,3},{2,0},{3,1},{4,6},{5,7},{6,4},{7,5},{8,10},{9,11},{10,... | collective-permute-start | bytes 1572872 | tf_op jit(solution)/shard_map/ppermute | solution.py:492
  13.5 27.1 %collective-permute-start = (bf16[256,256]{1,0:T(8,128)(2,1)S(1)}, bf16[256,256]{1,0:T(8,128)(2,1)S(1)}, u32[]{:S(2)}, u32[]{:S(2)}) collective-permute-start(bf16[256,256]{1,0:T(8,128)(2,1)S(1)} %bitcast.195), channel_id=1, source_target_pairs={{0,8},{8,16},{16,24},{24,0},{1,9},{9,17},{17,25},{25,1},{2,10},{10... | collective-permute-start | bytes 393224 | tf_op jit(solution)/shard_map/ppermute | solution.py:463
  15.6 25.0 %collective-permute-start.1 = (bf16[256,256]{1,0:T(8,128)(2,1)S(1)}, bf16[256,256]{1,0:T(8,128)(2,1)S(1)}, u32[]{:S(2)}, u32[]{:S(2)}) collective-permute-start(bf16[256,256]{1,0:T(8,128)(2,1)S(1)} %bitcast.196), channel_id=1, source_target_pairs={{0,16},{8,24},{16,0},{24,8},{1,17},{9,25},{17,1},{25,9},{2,18},{10... | collective-permute-start | bytes 393224 | tf_op jit(solution)/shard_map/ppermute | solution.py:463
  26.4 0.6 copy-start.8
  37.3 7.6 %copy-start.13 = (bf16[256,1024]{1,0:T(8,128)(2,1)}, bf16[256,1024]{1,0:T(8,128)(2,1)S(1)}, u32[]{:S(2)}) copy-start(bf16[256,1024]{1,0:T(8,128)(2,1)S(1)} %collective-permute-done.5) | copy-start | bytes 1572868
  37.3 5.0 collective-permute-start.2
  39.3 5.7 copy-start.14
  39.9 5.0 copy-start.15
  40.6 1.7 copy-start.18
  40.6 1.7 copy-start.19
  42.3 0.7 copy-start.23
  44.9 4.8 copy-start.3
  44.9 4.9 copy-start.25
  44.9 80.3 %all-to-all-start = ((bf16[8,70,32,128]{3,2,1,0:T(8,128)(2,1)}), bf16[8,70,32,128]{3,2,1,0:T(8,128)(2,1)}, u32[]{:S(2)}, u32[]{:S(2)}) async-start(bf16[8,70,32,128]{3,2,1,0:T(8,128)(2,1)} %bitcast.160), calls=%async_computation | async-start | bytes 9175040 | tf_op jit(solution)/shard_map/all_to_all | solution.py:480
  49.7 214.7 %reduce-scatter.6.cloned.1.call-start = ((), (), s32[]{:S(2)}) async-start(), calls=%async_computation.10 | async-start | bytes 5242880 | tf_op jit(solution)/shard_map/reduce_scatter | solution.py:517
  53.0 243.2 %copy-start = (bf16[4,256,1024]{2,1,0:T(8,128)(2,1)}, bf16[4,256,1024]{2,1,0:T(8,128)(2,1)S(1)}, u32[]{:S(2)}) copy-start(bf16[4,256,1024]{2,1,0:T(8,128)(2,1)S(1)} %pad_maximum_fusion.1.refs_0_) | copy-start | bytes 6291460
  54.1 23.5 %collective-permute-start.8 = (bf16[352,1024]{1,0:T(8,128)(2,1)}, bf16[352,1024]{1,0:T(8,128)(2,1)S(1)}, u32[]{:S(2)}, u32[]{:S(2)}) collective-permute-start(bf16[352,1024]{1,0:T(8,128)(2,1)} %pad_maximum_fusion.4), channel_id=1, source_target_pairs={{0,24},{8,0},{16,8},{24,16},{1,25},{9,1},{17,9},{25,17},{2,26},{10... | collective-permute-start | bytes 2162696 | tf_op jit(solution)/shard_map/ppermute | solution.py:463
  57.7 60.7 %collective-permute-start.7 = (bf16[352,1024]{1,0:T(8,128)(2,1)}, bf16[352,1024]{1,0:T(8,128)(2,1)S(1)}, u32[]{:S(2)}, u32[]{:S(2)}) collective-permute-start(bf16[352,1024]{1,0:T(8,128)(2,1)} %pad_maximum_fusion.4), channel_id=1, source_target_pairs={{0,16},{8,24},{16,0},{24,8},{1,17},{9,25},{17,1},{25,9},{2,18},{10... | collective-permute-start | bytes 2162696 | tf_op jit(solution)/shard_map/ppermute | solution.py:463
  62.1 56.9 %collective-permute-start.6 = (bf16[352,1024]{1,0:T(8,128)(2,1)}, bf16[352,1024]{1,0:T(8,128)(2,1)S(1)}, u32[]{:S(2)}, u32[]{:S(2)}) collective-permute-start(bf16[352,1024]{1,0:T(8,128)(2,1)} %pad_maximum_fusion.4), channel_id=1, source_target_pairs={{0,8},{8,16},{16,24},{24,0},{1,9},{9,17},{17,25},{25,1},{2,10},{10... | collective-permute-start | bytes 2162696 | tf_op jit(solution)/shard_map/ppermute | solution.py:463
  77.5 71.3 %copy-start.10 = (bf16[352,1024]{1,0:T(8,128)(2,1)}, bf16[352,1024]{1,0:T(8,128)(2,1)S(1)}, u32[]{:S(2)}) copy-start(bf16[352,1024]{1,0:T(8,128)(2,1)S(1)} %collective-permute-done.8) | copy-start | bytes 2162692
  118.4 30.5 %copy-start.11 = (bf16[352,1024]{1,0:T(8,128)(2,1)}, bf16[352,1024]{1,0:T(8,128)(2,1)S(1)}, u32[]{:S(2)}) copy-start(bf16[352,1024]{1,0:T(8,128)(2,1)S(1)} %collective-permute-done.7) | copy-start | bytes 2162692
  119.0 0.9 copy-start.12
  144.2 121.5 %all-to-all-start.1 = ((bf16[8,70,32,128]{3,2,1,0:T(8,128)(2,1)}), bf16[8,70,32,128]{3,2,1,0:T(8,128)(2,1)}, u32[]{:S(2)}, u32[]{:S(2)}) async-start(bf16[8,70,32,128]{3,2,1,0:T(8,128)(2,1)} %tie.5), calls=%async_computation.1 | async-start | bytes 9175040 | tf_op jit(solution)/shard_map/all_to_all | solution.py:480
  148.8 221.3 %reduce-scatter.8.cloned.1.call-start = ((), (), s32[]{:S(2)}) async-start(), calls=%async_computation.11 | async-start | bytes 5242880 | tf_op jit(solution)/shard_map/reduce_scatter | solution.py:529
  151.3 79.8 %collective-permute-start.9 = (bf16[3,224,1024]{2,1,0:T(8,128)(2,1)}, bf16[3,224,1024]{2,1,0:T(8,128)(2,1)S(1)}, u32[]{:S(2)}, u32[]{:S(2)}) collective-permute-start(bf16[3,224,1024]{2,1,0:T(8,128)(2,1)} %tie.4), channel_id=1, source_target_pairs={{0,2},{1,3},{2,0},{3,1},{4,6},{5,7},{6,4},{7,5},{8,10},{9,11},{10,... | collective-permute-start | bytes 4128776 | tf_op jit(solution)/shard_map/ppermute | solution.py:492
  153.2 107.9 %collective-permute-start.11 = (bf16[3,224,1024]{2,1,0:T(8,128)(2,1)}, bf16[3,224,1024]{2,1,0:T(8,128)(2,1)S(1)}, u32[]{:S(2)}, u32[]{:S(2)}) collective-permute-start(bf16[3,224,1024]{2,1,0:T(8,128)(2,1)} %tie.4), channel_id=1, source_target_pairs={{0,6},{1,7},{2,4},{3,5},{4,2},{5,3},{6,0},{7,1},{8,14},{9,15},{10,... | collective-permute-start | bytes 4128776 | tf_op jit(solution)/shard_map/ppermute | solution.py:492
  154.6 108.1 %collective-permute-start.10 = (bf16[3,224,1024]{2,1,0:T(8,128)(2,1)}, bf16[3,224,1024]{2,1,0:T(8,128)(2,1)S(1)}, u32[]{:S(2)}, u32[]{:S(2)}) collective-permute-start(bf16[3,224,1024]{2,1,0:T(8,128)(2,1)} %tie.4), channel_id=1, source_target_pairs={{0,4},{1,5},{2,6},{3,7},{4,0},{5,1},{6,2},{7,3},{8,12},{9,13},{10,... | collective-permute-start | bytes 4128776 | tf_op jit(solution)/shard_map/ppermute | solution.py:492
  231.1 1.2 copy-start.4
  261.1 1.0 copy-start.5
  262.7 1.1 copy-start.6
  283.5 1.3 copy-start.1
  290.1 14.1 %collective-permute-start.14 = (bf16[4,3,224,1024]{3,2,1,0:T(8,128)(2,1)}, bf16[4,3,224,1024]{3,2,1,0:T(8,128)(2,1)}, u32[]{:S(2)}, u32[]{:S(2)}) collective-permute-start(bf16[4,3,224,1024]{3,2,1,0:T(8,128)(2,1)} %pad_maximum_fusion.refs_2_), channel_id=1, source_target_pairs={{0,1},{1,0},{2,3},{3,2},{4,5},{5,4},{6,7},{7,6},{8,9},{9,8},{10,11... | collective-permute-start | bytes 16515080 | tf_op jit(solution)/shard_map/ppermute | solution.py:531
  291.4 57.9 %all-to-all-start.2 = ((bf16[8,70,32,128]{3,2,1,0:T(8,128)(2,1)}), bf16[8,70,32,128]{3,2,1,0:T(8,128)(2,1)}, u32[]{:S(2)}, u32[]{:S(2)}) async-start(bf16[8,70,32,128]{3,2,1,0:T(8,128)(2,1)} %tie.6), calls=%async_computation.2 | async-start | bytes 9175040 | tf_op jit(solution)/shard_map/all_to_all | solution.py:480
  296.0 159.8 %all-gather.8.cloned.1.call-start = ((), (), s32[]{:S(2)}) async-start(), calls=%async_computation.13 | async-start | bytes 5242880 | tf_op jit(solution)/shard_map/all_gather | solution.py:546
  296.3 8.0 %collective-permute-start.12 = (bf16[4,256,1024]{2,1,0:T(8,128)(2,1)S(1)}, bf16[4,256,1024]{2,1,0:T(8,128)(2,1)}, u32[]{:S(2)}, u32[]{:S(2)}) collective-permute-start(bf16[4,256,1024]{2,1,0:T(8,128)(2,1)S(1)} %pad_maximum_fusion.1.refs_0_), channel_id=1, source_target_pairs={{0,1},{1,0},{2,3},{3,2},{4,5},{5,4},{6,7},{7,6},{8,9},{9,8},{10,11... | collective-permute-start | bytes 6291464 | tf_op jit(solution)/shard_map/ppermute | solution.py:531
  299.8 49.6 %copy-start.2 = (bf16[3,4,32,1024]{3,2,1,0:T(8,128)(2,1)}, bf16[3,4,32,1024]{3,2,1,0:T(8,128)(2,1)S(1)}, u32[]{:S(2)}) copy-start(bf16[3,4,32,1024]{3,2,1,0:T(8,128)(2,1)S(1)} %pad_maximum_fusion.3.refs_1_) | copy-start | bytes 2359300
  299.8 4.4 collective-permute-start.13
  349.4 20.7 %copy-start.7 = (bf16[1,16,32,1024]{3,2,1,0:T(8,128)(2,1)S(1)}, bf16[1,16,32,1024]{3,2,1,0:T(8,128)(2,1)}, u32[]{:S(2)}) copy-start(bf16[1,16,32,1024]{3,2,1,0:T(8,128)(2,1)} %reduce-scatter.6.cloned.1.call-done) | copy-start | bytes 3145732
  394.9 58.0 %all-to-all-start.3 = ((bf16[8,70,32,128]{3,2,1,0:T(8,128)(2,1)}), bf16[8,70,32,128]{3,2,1,0:T(8,128)(2,1)}, u32[]{:S(2)}, u32[]{:S(2)}) async-start(bf16[8,70,32,128]{3,2,1,0:T(8,128)(2,1)} %bitcast.162), calls=%async_computation.5 | async-start | bytes 9175040 | tf_op jit(solution)/shard_map/all_to_all | solution.py:543
  399.6 137.0 %all-gather.6.cloned.1.call-start = ((), (), s32[]{:S(2)}) async-start(), calls=%async_computation.12 | async-start | bytes 5242880 | tf_op jit(solution)/shard_map/all_gather | solution.py:550
  473.0 4.8 copy-start.17
  473.0 5.1 copy-start.9
  473.0 58.1 %all-to-all-start.4 = ((bf16[8,70,32,128]{3,2,1,0:T(8,128)(2,1)}), bf16[8,70,32,128]{3,2,1,0:T(8,128)(2,1)}, u32[]{:S(2)}, u32[]{:S(2)}) async-start(bf16[8,70,32,128]{3,2,1,0:T(8,128)(2,1)} %bitcast.161), calls=%async_computation.6 | async-start | bytes 9175040 | tf_op jit(solution)/shard_map/all_to_all | solution.py:543
  477.8 121.0 %reduce-scatter.10.cloned.1.call-start = ((), (), s32[]{:S(2)}) async-start(), calls=%async_computation.14 | async-start | bytes 2621440
  551.1 4.4 collective-permute-start.15
  577.8 63.6 %all-to-all-start.5 = ((bf16[8,70,32,128]{3,2,1,0:T(8,128)(2,1)}), bf16[8,70,32,128]{3,2,1,0:T(8,128)(2,1)}, u32[]{:S(2)}, u32[]{:S(2)}) async-start(bf16[8,70,32,128]{3,2,1,0:T(8,128)(2,1)} %bitcast.163), calls=%async_computation.7 | async-start | bytes 9175040 | tf_op jit(solution)/shard_map/all_to_all | solution.py:543
  603.0 43.8 %collective-permute-start.16 = (bf16[256,256]{1,0:T(8,128)(2,1)S(1)}, bf16[256,256]{1,0:T(8,128)(2,1)S(1)}, u32[]{:S(2)}, u32[]{:S(2)}) collective-permute-start(bf16[256,256]{1,0:T(8,128)(2,1)S(1)} %get-tuple-element.33), channel_id=1, source_target_pairs={{0,8},{8,16},{16,24},{24,0},{1,9},{9,17},{17,25},{25,1},{2,10},{10... | collective-permute-start | bytes 393224 | tf_op jit(solution)/shard_map/ppermute | solution.py:463
  604.7 42.2 %collective-permute-start.17 = (bf16[256,256]{1,0:T(8,128)(2,1)S(1)}, bf16[256,256]{1,0:T(8,128)(2,1)S(1)}, u32[]{:S(2)}, u32[]{:S(2)}) collective-permute-start(bf16[256,256]{1,0:T(8,128)(2,1)S(1)} %get-tuple-element.32), channel_id=1, source_target_pairs={{0,16},{8,24},{16,0},{24,8},{1,17},{9,25},{17,1},{25,9},{2,18},{10... | collective-permute-start | bytes 393224 | tf_op jit(solution)/shard_map/ppermute | solution.py:463
  607.1 39.8 %collective-permute-start.18 = (bf16[256,256]{1,0:T(8,128)(2,1)S(1)}, bf16[256,256]{1,0:T(8,128)(2,1)S(1)}, u32[]{:S(2)}, u32[]{:S(2)}) collective-permute-start(bf16[256,256]{1,0:T(8,128)(2,1)S(1)} %get-tuple-element.31), channel_id=1, source_target_pairs={{0,24},{8,0},{16,8},{24,16},{1,25},{9,1},{17,9},{25,17},{2,26},{10... | collective-permute-start | bytes 393224 | tf_op jit(solution)/shard_map/ppermute | solution.py:463
  646.8 0.7 copy-start.20
  646.8 0.7 copy-start.21
  646.8 0.7 copy-start.22
Sparse Core Ops, SparseCore 0:
  45.0 63.0 all-gather.3
  143.1 78.2 reduce-scatter.5
  283.6 76.2 reduce-scatter.7
  375.5 80.2 all-gather.7
  457.2 79.2 all-gather.5
  559.5 39.2 reduce-scatter.9
where the time goes:
time: 661 us; the launch traced here: 658 us
  waiting for transfers between devices  324 us (49%)
  Pallas kernels  178 us (27%)
  local copies, waits for them, and re-layouts  60.4 us (9%)
  starting transfers between devices  52.4 us (8%)
  other arithmetic  29.7 us (4%)
  between operations  14.7 us (2%)
    all_to_all x3, waiting for transfers between devices, give_back(): lax.all_to_all(leaving, 'own', split_axis=0, concat_axis=0, tiled=True)  109 us
    ppermute x6, waiting for transfers between devices, over_chips(): return [value] + [lax.ppermute(value, 'own', turn) for turn in turns]  105 us
    all_to_all x3, waiting for transfers between devices, receive(): lax.all_to_all(sending, 'own', split_axis=0, concat_axis=0, tiled=True)  45.1 us
    ppermute x9, waiting for transfers between devices, exchange(): kept.append(lax.ppermute(parts[s], 'dp', turn))  41.9 us
    pallas_call x2, Pallas kernels, forward(): pl.pallas_call(kernel, out_shape=(jax.ShapeDtypeStruct((row_blocks, rows_...  35.4 us
    pallas_call x2, Pallas kernels, weight_grad(): pl.pallas_call(kernel, out_shape=jax.ShapeDtypeStruct((places, rows_each,...  34.4 us
    pallas_call x2, Pallas kernels, input_part(): pl.pallas_call(kernel, out_shape=(out, out), grid_spec=pltpu.PrefetchScal...  28.5 us
    squeeze x21, local copies, waits for them, and re-layouts, mark(): return value.reshape((-1,) + value.shape[-2:])[0, :16, :128]  20.8 us
  transfers between devices with their start and end apart: 31, of which 13 were waited for; matrix products, arithmetic and copies ran while one was open for 11% of the time, Pallas kernels for 19%

commit v1 on v0

--- a/solution.py
+++ b/solution.py
@@ -348,7 +348,7 @@
     )(first, weights, weights, grad, *earlier, *after)
 
 
-def unpack(which, returned, source, total):
+def unpack(which, returned, source, total, after=()):
     places, rows_each, block = returned.shape
     slot_count = source.shape[0]
 
@@ -369,14 +369,14 @@
         grid_spec=pltpu.PrefetchScalarGridSpec(
             num_scalar_prefetch=1,
             grid=(1,),
-            in_specs=[whole((places, rows_each, block))] + waiting(extra),
+            in_specs=[whole((places, rows_each, block))] + waiting(extra) + waiting(after),
             out_specs=pl.BlockSpec((1,) + shape[1:], lambda g, s: (which, 0, 0, 0)),
         ),
         input_output_aliases={2: 0} if extra else {},
         compiler_params=PARAMS,
         cost_estimate=COST,
         name="unpack",
-    )(source, returned, *extra)
+    )(source, returned, *extra, *after)
 
 
 def in_order(kept, quarter, after=()):
@@ -574,7 +574,7 @@
     back = in_order(exchange(to_planes(back)), quarter)
     back = back.reshape(data_count, row_blocks // own_count, rows_each, local_tokens)
     input_grad = back.transpose(3, 1, 0, 2).reshape(local_tokens, local_width)
-    total = unpack(0, returned, source[0], total)
+    total = unpack(0, returned, source[0], total, (mark(input_grad),))
     return (input_grad, total)
 
 

time: 661 us -> 656 us (level)
    all_to_all x3, waiting for transfers between devices: 109 us -> 95.7 us  [give_back(): lax.all_to_all(leaving, 'own', split_axis=0, concat_axis=0, tiled=True)]
    ppermute x9, waiting for transfers between devices: 41.9 us -> 49.4 us  [exchange(): kept.append(lax.ppermute(parts[s], 'dp', turn))]
  transfers between devices with their start and end apart: 31 -> 31, of which waited for: 13 -> 15; matrix products, arithmetic and copies ran while one was open for 11% -> 11% of each run, Pallas kernels for 19% -> 18%
where the time goes in v1:
time: 656 us; the launch traced here: 654 us
  waiting for transfers between devices  318 us (48%)
  Pallas kernels  178 us (27%)
  local copies, waits for them, and re-layouts  61 us (9%)
  starting transfers between devices  52.4 us (8%)
  other arithmetic  29.7 us (5%)
  between operations  14.7 us (2%)
    ppermute x6, waiting for transfers between devices, over_chips(): return [value] + [lax.ppermute(value, 'own', turn) for turn in turns]  105 us
    all_to_all x3, waiting for transfers between devices, give_back(): lax.all_to_all(leaving, 'own', split_axis=0, concat_axis=0, tiled=True)  95.7 us
    ppermute x9, waiting for transfers between devices, exchange(): kept.append(lax.ppermute(parts[s], 'dp', turn))  49.4 us
    all_to_all x3, waiting for transfers between devices, receive(): lax.all_to_all(sending, 'own', split_axis=0, concat_axis=0, tiled=True)  45.1 us
    pallas_call x2, Pallas kernels, forward(): pl.pallas_call(kernel, out_shape=(jax.ShapeDtypeStruct((row_blocks, rows_...  35.4 us
    pallas_call x2, Pallas kernels, weight_grad(): pl.pallas_call(kernel, out_shape=jax.ShapeDtypeStruct((places, rows_each,...  34.4 us
    pallas_call x2, Pallas kernels, input_part(): pl.pallas_call(kernel, out_shape=(out, out), grid_spec=pltpu.PrefetchScal...  28.5 us
    squeeze x21, local copies, waits for them, and re-layouts, mark(): return value.reshape((-1,) + value.shape[-2:])[0, :16, :128]  20.8 us
  transfers between devices with their start and end apart: 31, of which 15 were waited for; matrix products, arithmetic and copies ran while one was open for 11% of the time, Pallas kernels for 18%

profile of v1, /device:TPU:0, one launch (start us, length us, event | category | flops | bytes accessed | tf_op | source)
XLA Modules:
  0.0 653.6 jit_solution(11166667437713115215)
XLA Ops:
  7.2 4.0 collective-permute-start.5
  13.5 2.0 collective-permute-start
  15.6 2.7 collective-permute-start.1
  18.6 3.4 reduce-window.6
  22.7 3.6 select_reduce_fusion.1
  29.0 6.2 pack.3
  37.3 1.3 collective-permute-start.2
  40.6 1.7 collective-permute-done.2.refs_3_
  42.9 1.9 in_order.2
  44.9 4.7 all-to-all-start
  51.3 1.7 pad_maximum_fusion.1.refs_0_
  54.1 3.1 collective-permute-start.8
  57.7 1.4 constant_dynamic-slice_fusion.2
  63.9 6.1 pack.4
  70.0 6.2 pack.5
  76.3 1.3 slice_bitcast_fusion.16
  78.2 40.2 %collective-permute-done.7 = bf16[352,1024]{1,0:T(8,128)(2,1)S(1)} collective-permute-done((bf16[352,1024]{1,0:T(8,128)(2,1)}, bf16[352,1024]{1,0:T(8,128)(2,1)S(1)}, u32[]{:S(2)}, u32[]{:S(2)}) %collective-permute-start.7) | collective-permute-done | bytes 720928 | tf_op jit(solution)/shard_map/ppermute | solution.py:463
  120.5 4.8 copy.88
  125.2 17.7 %forward.2 = (bf16[64,32,2048]{2,1,0:T(8,128)(2,1)}, bf16[4,16,32,1024]{3,2,1,0:T(8,128)(2,1)}) custom-call(s32[416]{0:T(512)} %bitcast.209, s32[416]{0:T(512)} %bitcast.207, bf16[1024,2048]{1,0:T(8,128)(2,1)} %bitcast.155, bf16[560,32,128]{2,1,0:T(8,128)(2,1)} %bitcast.24.arrived, bf16[16,128]{1,0:T(8,128)(2,1)} %get-tuple-element.57.refs_0_, ...), custom_call_target="tpu_custom_call" | custom-call | flops 1024 | bytes 1024 | tf_op jit(solution)/shard_map/forward/pallas_call | solution.py:106
  144.2 4.6 all-to-all-start.1
  150.0 1.3 pad_maximum_fusion.2.refs_0_
  151.3 1.9 collective-permute-start.9
  153.2 1.5 collective-permute-start.11
  154.8 76.3 %collective-permute-done.9 = bf16[3,224,1024]{2,1,0:T(8,128)(2,1)S(1)} collective-permute-done((bf16[3,224,1024]{2,1,0:T(8,128)(2,1)}, bf16[3,224,1024]{2,1,0:T(8,128)(2,1)S(1)}, u32[]{:S(2)}, u32[]{:S(2)}) %collective-permute-start.9) | collective-permute-done | bytes 1376288 | tf_op jit(solution)/shard_map/ppermute | solution.py:492
  232.9 28.2 %collective-permute-done.11 = bf16[3,224,1024]{2,1,0:T(8,128)(2,1)S(1)} collective-permute-done((bf16[3,224,1024]{2,1,0:T(8,128)(2,1)}, bf16[3,224,1024]{2,1,0:T(8,128)(2,1)S(1)}, u32[]{:S(2)}, u32[]{:S(2)}) %collective-permute-start.11) | collective-permute-done | bytes 1376288 | tf_op jit(solution)/shard_map/ppermute | solution.py:492
  264.4 1.3 slice_bitcast_fusion.11.refs_0_
  265.7 17.7 %forward.3 = (bf16[64,32,2048]{2,1,0:T(8,128)(2,1)}, bf16[4,16,32,1024]{3,2,1,0:T(8,128)(2,1)}) custom-call(s32[416]{0:T(512)} %bitcast.213, s32[416]{0:T(512)} %bitcast.211, bf16[1024,2048]{1,0:T(8,128)(2,1)} %bitcast.156, bf16[560,32,128]{2,1,0:T(8,128)(2,1)} %bitcast.54.arrived, bf16[16,128]{1,0:T(8,128)(2,1)} %slice_bitcast_fusion.11.refs_0_, ...), custom_call_target="tpu_custom_call" | custom-call | flops 1024 | bytes 1024 | tf_op jit(solution)/shard_map/forward/pallas_call | solution.py:106
  283.5 1.3 copy-done.1
  284.8 5.3 pad_maximum_fusion.refs_2_
  290.1 1.3 slice_bitcast_fusion.12.refs_1_
  291.4 4.6 all-to-all-start.2
  300.6 3.6 collective-permute-done.13.refs_4_
  304.3 45.1 %all-to-all-done.2 = bf16[8,70,32,128]{3,2,1,0:T(8,128)(2,1)} async-done(((bf16[8,70,32,128]{3,2,1,0:T(8,128)(2,1)}), bf16[8,70,32,128]{3,2,1,0:T(8,128)(2,1)}, u32[]{:S(2)}, u32[]{:S(2)}) %all-to-all-start.2) | async-done | bytes 4587552 | tf_op jit(solution)/shard_map/all_to_all | solution.py:480
  349.4 20.7 %forward_down.1 = f32[512,1024]{1,0:T(8,128)} custom-call(s32[416]{0:T(512)} %bitcast.205, s32[416]{0:T(512)} %bitcast.203, s32[1]{0:T(128)} %bitcast.quarter, s32[8]{0:T(128)} %reshape.209.order, bf16[4,256,1024]{2,1,0:T(8,128)(2,1)} %copy-done, bf16[3,4,32,1024]{3,2,1,0:T(8,128)(2,1)} %copy-done.2, bf16[4,3,224,1024]{3,2,1,0:T(8,128)(2,1)} %pad_maximum_fusion.refs_2_, ...), custom_call_target="tpu_custom_call" | custom-call | flops 1024 | bytes 1024 | tf_op jit(solution)/shard_map/forward_down/pallas_call | solution.py:187
  370.1 5.3 multiply_convert_fusion
  375.4 19.6 %weight_grad_down.1 = bf16[560,32,128]{2,1,0:T(8,128)(2,1)} custom-call(s32[416]{0:T(512)} %bitcast.206, s32[416]{0:T(512)} %bitcast.204, s32[1]{0:T(128)} %bitcast.quarter, s32[8]{0:T(128)} %reshape.209.order, bf16[512,1024]{1,0:T(8,128)(2,1)} %get-tuple-element.30.value, bf16[4,256,1024]{2,1,0:T(8,128)(2,1)} %copy-done, ...), custom_call_target="tpu_custom_call" | custom-call | flops 1024 | bytes 1024 | tf_op jit(solution)/shard_map/weight_grad_down/pallas_call | solution.py:284
  394.9 4.6 all-to-all-start.3
  400.2 6.5 copy.80
  406.6 46.3 %all-to-all-done.3 = bf16[8,70,32,128]{3,2,1,0:T(8,128)(2,1)} async-done(((bf16[8,70,32,128]{3,2,1,0:T(8,128)(2,1)}), bf16[8,70,32,128]{3,2,1,0:T(8,128)(2,1)}, u32[]{:S(2)}, u32[]{:S(2)}) %all-to-all-start.3) | async-done | bytes 4587552 | tf_op jit(solution)/shard_map/all_to_all | solution.py:543
  452.9 1.3 slice_bitcast_fusion.7.refs_0_
  454.2 1.6 all-gather.8.cloned.1.call-done.grad
  455.8 17.2 %weight_grad.2 = bf16[560,32,128]{2,1,0:T(8,128)(2,1)} custom-call(s32[416]{0:T(512)} %bitcast.214, s32[416]{0:T(512)} %bitcast.212, bf16[2048,1024]{1,0:T(8,128)(2,1)} %bitcast.157, bf16[4,16,32,1024]{3,2,1,0:T(8,128)(2,1)} %all-gather.8.cloned.1.call-done.grad, bf16[16,128]{1,0:T(8,128)(2,1)} %slice_bitcast_fusion.7.refs_0_), custom_call_target="tpu_custom_call" | custom-call | flops 1024 | bytes 1024 | tf_op jit(solution)/shard_map/weight_grad/pallas_call | solution.py:230
  473.0 4.7 all-to-all-start.4
  479.7 5.5 unpack.3.refs_0_
  487.7 13.9 %input_part.2 = (f32[4,256,1024]{2,1,0:T(8,128)}, f32[4,256,1024]{2,1,0:T(8,128)}) custom-call(s32[1]{0:T(128)} %bitcast.1.first, bf16[2048,2048]{1,0:T(8,128)(2,1)} %bitcast.161, bf16[2048,2048]{1,0:T(8,128)(2,1)} %bitcast.162, bf16[4,16,32,1024]{3,2,1,0:T(8,128)(2,1)} %all-gather.8.cloned.1.call-done.grad, bf16[16,128]{1,0:T(8,128)(2,1)} %slice_bitcast_fusion.6.refs_0_), custom_call_target="tpu_custom_call" | custom-call | flops 1024 | bytes 1024 | tf_op jit(solution)/shard_map/input_part/pallas_call | solution.py:329
  501.7 29.4 %all-to-all-done.4 = bf16[8,70,32,128]{3,2,1,0:T(8,128)(2,1)} async-done(((bf16[8,70,32,128]{3,2,1,0:T(8,128)(2,1)}), bf16[8,70,32,128]{3,2,1,0:T(8,128)(2,1)}, u32[]{:S(2)}, u32[]{:S(2)}) %all-to-all-start.4) | async-done | bytes 4587552 | tf_op jit(solution)/shard_map/all_to_all | solution.py:543
  532.4 4.1 all-gather.6.cloned.1.call-done.grad
  536.5 14.5 %input_part.3 = (bf16[4,256,1024]{2,1,0:T(8,128)(2,1)}, bf16[4,256,1024]{2,1,0:T(8,128)(2,1)}) custom-call(s32[1]{0:T(128)} %bitcast.1.first, bf16[2048,2048]{1,0:T(8,128)(2,1)} %bitcast.159, bf16[2048,2048]{1,0:T(8,128)(2,1)} %bitcast.160, bf16[4,16,32,1024]{3,2,1,0:T(8,128)(2,1)} %all-gather.6.cloned.1.call-done.grad, ...), custom_call_target="tpu_custom_call" | custom-call | flops 1024 | bytes 1024 | tf_op jit(solution)/shard_map/input_part/pallas_call | solution.py:329
  551.1 4.4 collective-permute-done.15
  555.5 3.9 add_convert_fusion
  560.6 17.2 %weight_grad.3 = bf16[560,32,128]{2,1,0:T(8,128)(2,1)} custom-call(s32[416]{0:T(512)} %bitcast.210, s32[416]{0:T(512)} %bitcast.208, bf16[2048,1024]{1,0:T(8,128)(2,1)} %bitcast.158, bf16[4,16,32,1024]{3,2,1,0:T(8,128)(2,1)} %all-gather.6.cloned.1.call-done.grad, bf16[16,128]{1,0:T(8,128)(2,1)} %slice_bitcast_fusion.23.refs_0_), custom_call_target="tpu_custom_call" | custom-call | flops 1024 | bytes 1024 | tf_op jit(solution)/shard_map/weight_grad/pallas_call | solution.py:230
  577.8 4.6 all-to-all-start.5
  582.4 5.8 unpack.4.refs_0_
  588.2 1.3 slice_bitcast_fusion.3.refs_1_
  589.5 9.3 %reduce-scatter.10.cloned.1.call-done = bf16[1,256,1024]{2,1,0:T(8,128)(2,1)} async-done(((bf16[4,256,1024]{2,1,0:T(8,128)(2,1)}), bf16[1,256,1024]{2,1,0:T(8,128)(2,1)}) %reduce-scatter.10.cloned.1.call-update) | async-done | bytes 524304
  601.0 1.9 fusion.21
  603.0 1.7 collective-permute-start.16
  604.7 2.4 collective-permute-start.17
  607.1 1.4 collective-permute-start.18
  608.5 2.7 collective-permute-done.16.refs_1_
  611.2 4.7 collective-permute-done.17.refs_2_
  616.7 1.9 in_order.3
  621.4 20.0 %all-to-all-done.5 = bf16[8,70,32,128]{3,2,1,0:T(8,128)(2,1)} async-done(((bf16[8,70,32,128]{3,2,1,0:T(8,128)(2,1)}), bf16[8,70,32,128]{3,2,1,0:T(8,128)(2,1)}, u32[]{:S(2)}, u32[]{:S(2)}) %all-to-all-start.5) | async-done | bytes 4587552 | tf_op jit(solution)/shard_map/all_to_all | solution.py:543
  641.4 5.4 unpack.5
  (170 shorter events, 47.0 us)
Async XLA Ops:
  7.2 11.1 %copy-start.16 = (s32[3,128,26]{1,2,0:T(8,128)S(1)}, s32[3,128,26]{1,2,0:T(8,128)}, u32[]{:S(2)}) copy-start(s32[3,128,26]{1,2,0:T(8,128)} %param.12) | copy-start | bytes 119812
  7.2 15.3 %copy-start.24 = (s32[3,128,26]{1,2,0:T(8,128)S(1)}, s32[3,128,26]{1,2,0:T(8,128)}, u32[]{:S(2)}) copy-start(s32[3,128,26]{1,2,0:T(8,128)} %param.13) | copy-start | bytes 119812
  7.2 20.5 %copy-start.26 = (f32[3,416]{1,0:T(4,128)S(1)}, f32[3,416]{1,0:T(4,128)}, u32[]{:S(2)}) copy-start(f32[3,416]{1,0:T(4,128)} %param.10) | copy-start | bytes 14980
  7.2 113.3 %all-gather.4.cloned.1.call-start = ((), (), s32[]{:S(2)}) async-start(), calls=%async_computation.9 | async-start | bytes 4718592 | tf_op jit(solution)/shard_map/all_gather | solution.py:509
  7.2 30.1 %collective-permute-start.5 = (bf16[256,1024]{1,0:T(8,128)(2,1)}, bf16[256,1024]{1,0:T(8,128)(2,1)S(1)}, u32[]{:S(2)}, u32[]{:S(2)}) collective-permute-start(bf16[256,1024]{1,0:T(8,128)(2,1)} %param.8), channel_id=1, source_target_pairs={{0,6},{1,7},{2,4},{3,5},{4,2},{5,3},{6,0},{7,1},{8,14},{9,15},{10,... | collective-permute-start | bytes 1572872 | tf_op jit(solution)/shard_map/ppermute | solution.py:492
  11.2 28.1 %collective-permute-start.4 = (bf16[256,1024]{1,0:T(8,128)(2,1)}, bf16[256,1024]{1,0:T(8,128)(2,1)S(1)}, u32[]{:S(2)}, u32[]{:S(2)}) collective-permute-start(bf16[256,1024]{1,0:T(8,128)(2,1)} %param.8), channel_id=1, source_target_pairs={{0,4},{1,5},{2,6},{3,7},{4,0},{5,1},{6,2},{7,3},{8,12},{9,13},{10,... | collective-permute-start | bytes 1572872 | tf_op jit(solution)/shard_map/ppermute | solution.py:492
  11.7 28.2 %collective-permute-start.3 = (bf16[256,1024]{1,0:T(8,128)(2,1)}, bf16[256,1024]{1,0:T(8,128)(2,1)S(1)}, u32[]{:S(2)}, u32[]{:S(2)}) collective-permute-start(bf16[256,1024]{1,0:T(8,128)(2,1)} %param.8), channel_id=1, source_target_pairs={{0,2},{1,3},{2,0},{3,1},{4,6},{5,7},{6,4},{7,5},{8,10},{9,11},{10,... | collective-permute-start | bytes 1572872 | tf_op jit(solution)/shard_map/ppermute | solution.py:492
  13.5 27.1 %collective-permute-start = (bf16[256,256]{1,0:T(8,128)(2,1)S(1)}, bf16[256,256]{1,0:T(8,128)(2,1)S(1)}, u32[]{:S(2)}, u32[]{:S(2)}) collective-permute-start(bf16[256,256]{1,0:T(8,128)(2,1)S(1)} %bitcast.199), channel_id=1, source_target_pairs={{0,8},{8,16},{16,24},{24,0},{1,9},{9,17},{17,25},{25,1},{2,10},{10... | collective-permute-start | bytes 393224 | tf_op jit(solution)/shard_map/ppermute | solution.py:463
  15.6 25.0 %collective-permute-start.1 = (bf16[256,256]{1,0:T(8,128)(2,1)S(1)}, bf16[256,256]{1,0:T(8,128)(2,1)S(1)}, u32[]{:S(2)}, u32[]{:S(2)}) collective-permute-start(bf16[256,256]{1,0:T(8,128)(2,1)S(1)} %bitcast.200), channel_id=1, source_target_pairs={{0,16},{8,24},{16,0},{24,8},{1,17},{9,25},{17,1},{25,9},{2,18},{10... | collective-permute-start | bytes 393224 | tf_op jit(solution)/shard_map/ppermute | solution.py:463
  26.4 0.6 copy-start.8
  37.3 7.6 %copy-start.13 = (bf16[256,1024]{1,0:T(8,128)(2,1)}, bf16[256,1024]{1,0:T(8,128)(2,1)S(1)}, u32[]{:S(2)}) copy-start(bf16[256,1024]{1,0:T(8,128)(2,1)S(1)} %collective-permute-done.5) | copy-start | bytes 1572868
  37.3 5.0 collective-permute-start.2
  39.3 5.7 copy-start.14
  39.9 5.0 copy-start.15
  40.6 1.7 copy-start.18
  40.6 1.7 copy-start.19
  42.3 0.7 copy-start.20
  44.9 4.8 copy-start.3
  44.9 4.9 copy-start.25
  44.9 80.3 %all-to-all-start = ((bf16[8,70,32,128]{3,2,1,0:T(8,128)(2,1)}), bf16[8,70,32,128]{3,2,1,0:T(8,128)(2,1)}, u32[]{:S(2)}, u32[]{:S(2)}) async-start(bf16[8,70,32,128]{3,2,1,0:T(8,128)(2,1)} %bitcast.163), calls=%async_computation | async-start | bytes 9175040 | tf_op jit(solution)/shard_map/all_to_all | solution.py:480
  49.7 214.7 %reduce-scatter.6.cloned.1.call-start = ((), (), s32[]{:S(2)}) async-start(), calls=%async_computation.10 | async-start | bytes 5242880 | tf_op jit(solution)/shard_map/reduce_scatter | solution.py:517
  53.0 243.2 %copy-start = (bf16[4,256,1024]{2,1,0:T(8,128)(2,1)}, bf16[4,256,1024]{2,1,0:T(8,128)(2,1)S(1)}, u32[]{:S(2)}) copy-start(bf16[4,256,1024]{2,1,0:T(8,128)(2,1)S(1)} %pad_maximum_fusion.1.refs_0_) | copy-start | bytes 6291460
  54.1 23.5 %collective-permute-start.8 = (bf16[352,1024]{1,0:T(8,128)(2,1)}, bf16[352,1024]{1,0:T(8,128)(2,1)S(1)}, u32[]{:S(2)}, u32[]{:S(2)}) collective-permute-start(bf16[352,1024]{1,0:T(8,128)(2,1)} %pad_maximum_fusion.4), channel_id=1, source_target_pairs={{0,24},{8,0},{16,8},{24,16},{1,25},{9,1},{17,9},{25,17},{2,26},{10... | collective-permute-start | bytes 2162696 | tf_op jit(solution)/shard_map/ppermute | solution.py:463
  57.7 60.7 %collective-permute-start.7 = (bf16[352,1024]{1,0:T(8,128)(2,1)}, bf16[352,1024]{1,0:T(8,128)(2,1)S(1)}, u32[]{:S(2)}, u32[]{:S(2)}) collective-permute-start(bf16[352,1024]{1,0:T(8,128)(2,1)} %pad_maximum_fusion.4), channel_id=1, source_target_pairs={{0,16},{8,24},{16,0},{24,8},{1,17},{9,25},{17,1},{25,9},{2,18},{10... | collective-permute-start | bytes 2162696 | tf_op jit(solution)/shard_map/ppermute | solution.py:463
  62.1 56.9 %collective-permute-start.6 = (bf16[352,1024]{1,0:T(8,128)(2,1)}, bf16[352,1024]{1,0:T(8,128)(2,1)S(1)}, u32[]{:S(2)}, u32[]{:S(2)}) collective-permute-start(bf16[352,1024]{1,0:T(8,128)(2,1)} %pad_maximum_fusion.4), channel_id=1, source_target_pairs={{0,8},{8,16},{16,24},{24,0},{1,9},{9,17},{17,25},{25,1},{2,10},{10... | collective-permute-start | bytes 2162696 | tf_op jit(solution)/shard_map/ppermute | solution.py:463
  77.5 71.3 %copy-start.10 = (bf16[352,1024]{1,0:T(8,128)(2,1)}, bf16[352,1024]{1,0:T(8,128)(2,1)S(1)}, u32[]{:S(2)}) copy-start(bf16[352,1024]{1,0:T(8,128)(2,1)S(1)} %collective-permute-done.8) | copy-start | bytes 2162692
  118.4 30.5 %copy-start.11 = (bf16[352,1024]{1,0:T(8,128)(2,1)}, bf16[352,1024]{1,0:T(8,128)(2,1)S(1)}, u32[]{:S(2)}) copy-start(bf16[352,1024]{1,0:T(8,128)(2,1)S(1)} %collective-permute-done.7) | copy-start | bytes 2162692
  119.0 0.9 copy-start.12
  144.2 121.5 %all-to-all-start.1 = ((bf16[8,70,32,128]{3,2,1,0:T(8,128)(2,1)}), bf16[8,70,32,128]{3,2,1,0:T(8,128)(2,1)}, u32[]{:S(2)}, u32[]{:S(2)}) async-start(bf16[8,70,32,128]{3,2,1,0:T(8,128)(2,1)} %tie.5), calls=%async_computation.1 | async-start | bytes 9175040 | tf_op jit(solution)/shard_map/all_to_all | solution.py:480
  148.8 221.3 %reduce-scatter.8.cloned.1.call-start = ((), (), s32[]{:S(2)}) async-start(), calls=%async_computation.11 | async-start | bytes 5242880 | tf_op jit(solution)/shard_map/reduce_scatter | solution.py:529
  151.3 79.8 %collective-permute-start.9 = (bf16[3,224,1024]{2,1,0:T(8,128)(2,1)}, bf16[3,224,1024]{2,1,0:T(8,128)(2,1)S(1)}, u32[]{:S(2)}, u32[]{:S(2)}) collective-permute-start(bf16[3,224,1024]{2,1,0:T(8,128)(2,1)} %tie.4), channel_id=1, source_target_pairs={{0,2},{1,3},{2,0},{3,1},{4,6},{5,7},{6,4},{7,5},{8,10},{9,11},{10,... | collective-permute-start | bytes 4128776 | tf_op jit(solution)/shard_map/ppermute | solution.py:492
  153.2 107.9 %collective-permute-start.11 = (bf16[3,224,1024]{2,1,0:T(8,128)(2,1)}, bf16[3,224,1024]{2,1,0:T(8,128)(2,1)S(1)}, u32[]{:S(2)}, u32[]{:S(2)}) collective-permute-start(bf16[3,224,1024]{2,1,0:T(8,128)(2,1)} %tie.4), channel_id=1, source_target_pairs={{0,6},{1,7},{2,4},{3,5},{4,2},{5,3},{6,0},{7,1},{8,14},{9,15},{10,... | collective-permute-start | bytes 4128776 | tf_op jit(solution)/shard_map/ppermute | solution.py:492
  154.6 108.1 %collective-permute-start.10 = (bf16[3,224,1024]{2,1,0:T(8,128)(2,1)}, bf16[3,224,1024]{2,1,0:T(8,128)(2,1)S(1)}, u32[]{:S(2)}, u32[]{:S(2)}) collective-permute-start(bf16[3,224,1024]{2,1,0:T(8,128)(2,1)} %tie.4), channel_id=1, source_target_pairs={{0,4},{1,5},{2,6},{3,7},{4,0},{5,1},{6,2},{7,3},{8,12},{9,13},{10,... | collective-permute-start | bytes 4128776 | tf_op jit(solution)/shard_map/ppermute | solution.py:492
  231.1 1.2 copy-start.4
  261.1 1.0 copy-start.5
  262.7 1.1 copy-start.6
  283.5 1.3 copy-start.1
  290.1 14.1 %collective-permute-start.14 = (bf16[4,3,224,1024]{3,2,1,0:T(8,128)(2,1)}, bf16[4,3,224,1024]{3,2,1,0:T(8,128)(2,1)}, u32[]{:S(2)}, u32[]{:S(2)}) collective-permute-start(bf16[4,3,224,1024]{3,2,1,0:T(8,128)(2,1)} %pad_maximum_fusion.refs_2_), channel_id=1, source_target_pairs={{0,1},{1,0},{2,3},{3,2},{4,5},{5,4},{6,7},{7,6},{8,9},{9,8},{10,11... | collective-permute-start | bytes 16515080 | tf_op jit(solution)/shard_map/ppermute | solution.py:531
  291.4 57.9 %all-to-all-start.2 = ((bf16[8,70,32,128]{3,2,1,0:T(8,128)(2,1)}), bf16[8,70,32,128]{3,2,1,0:T(8,128)(2,1)}, u32[]{:S(2)}, u32[]{:S(2)}) async-start(bf16[8,70,32,128]{3,2,1,0:T(8,128)(2,1)} %tie.6), calls=%async_computation.2 | async-start | bytes 9175040 | tf_op jit(solution)/shard_map/all_to_all | solution.py:480
  296.0 159.8 %all-gather.8.cloned.1.call-start = ((), (), s32[]{:S(2)}) async-start(), calls=%async_computation.13 | async-start | bytes 5242880 | tf_op jit(solution)/shard_map/all_gather | solution.py:546
  296.3 8.0 %collective-permute-start.12 = (bf16[4,256,1024]{2,1,0:T(8,128)(2,1)S(1)}, bf16[4,256,1024]{2,1,0:T(8,128)(2,1)}, u32[]{:S(2)}, u32[]{:S(2)}) collective-permute-start(bf16[4,256,1024]{2,1,0:T(8,128)(2,1)S(1)} %pad_maximum_fusion.1.refs_0_), channel_id=1, source_target_pairs={{0,1},{1,0},{2,3},{3,2},{4,5},{5,4},{6,7},{7,6},{8,9},{9,8},{10,11... | collective-permute-start | bytes 6291464 | tf_op jit(solution)/shard_map/ppermute | solution.py:531
  299.8 49.6 %copy-start.2 = (bf16[3,4,32,1024]{3,2,1,0:T(8,128)(2,1)}, bf16[3,4,32,1024]{3,2,1,0:T(8,128)(2,1)S(1)}, u32[]{:S(2)}) copy-start(bf16[3,4,32,1024]{3,2,1,0:T(8,128)(2,1)S(1)} %pad_maximum_fusion.3.refs_1_) | copy-start | bytes 2359300
  299.8 4.4 collective-permute-start.13
  349.4 20.7 %copy-start.7 = (bf16[1,16,32,1024]{3,2,1,0:T(8,128)(2,1)S(1)}, bf16[1,16,32,1024]{3,2,1,0:T(8,128)(2,1)}, u32[]{:S(2)}) copy-start(bf16[1,16,32,1024]{3,2,1,0:T(8,128)(2,1)} %reduce-scatter.6.cloned.1.call-done) | copy-start | bytes 3145732
  394.9 58.0 %all-to-all-start.3 = ((bf16[8,70,32,128]{3,2,1,0:T(8,128)(2,1)}), bf16[8,70,32,128]{3,2,1,0:T(8,128)(2,1)}, u32[]{:S(2)}, u32[]{:S(2)}) async-start(bf16[8,70,32,128]{3,2,1,0:T(8,128)(2,1)} %bitcast.165), calls=%async_computation.5 | async-start | bytes 9175040 | tf_op jit(solution)/shard_map/all_to_all | solution.py:543
  399.6 137.0 %all-gather.6.cloned.1.call-start = ((), (), s32[]{:S(2)}) async-start(), calls=%async_computation.12 | async-start | bytes 5242880 | tf_op jit(solution)/shard_map/all_gather | solution.py:550
  473.0 4.8 copy-start.17
  473.0 5.1 copy-start.9
  473.0 58.1 %all-to-all-start.4 = ((bf16[8,70,32,128]{3,2,1,0:T(8,128)(2,1)}), bf16[8,70,32,128]{3,2,1,0:T(8,128)(2,1)}, u32[]{:S(2)}, u32[]{:S(2)}) async-start(bf16[8,70,32,128]{3,2,1,0:T(8,128)(2,1)} %bitcast.164), calls=%async_computation.6 | async-start | bytes 9175040 | tf_op jit(solution)/shard_map/all_to_all | solution.py:543
  477.8 121.0 %reduce-scatter.10.cloned.1.call-start = ((), (), s32[]{:S(2)}) async-start(), calls=%async_computation.14 | async-start | bytes 2621440
  551.1 4.4 collective-permute-start.15
  577.8 63.6 %all-to-all-start.5 = ((bf16[8,70,32,128]{3,2,1,0:T(8,128)(2,1)}), bf16[8,70,32,128]{3,2,1,0:T(8,128)(2,1)}, u32[]{:S(2)}, u32[]{:S(2)}) async-start(bf16[8,70,32,128]{3,2,1,0:T(8,128)(2,1)} %bitcast.166), calls=%async_computation.7 | async-start | bytes 9175040 | tf_op jit(solution)/shard_map/all_to_all | solution.py:543
  603.0 8.3 %collective-permute-start.16 = (bf16[256,256]{1,0:T(8,128)(2,1)S(1)}, bf16[256,256]{1,0:T(8,128)(2,1)S(1)}, u32[]{:S(2)}, u32[]{:S(2)}) collective-permute-start(bf16[256,256]{1,0:T(8,128)(2,1)S(1)} %get-tuple-element.33), channel_id=1, source_target_pairs={{0,8},{8,16},{16,24},{24,0},{1,9},{9,17},{17,25},{25,1},{2,10},{10... | collective-permute-start | bytes 393224 | tf_op jit(solution)/shard_map/ppermute | solution.py:463
  604.7 11.3 %collective-permute-start.17 = (bf16[256,256]{1,0:T(8,128)(2,1)S(1)}, bf16[256,256]{1,0:T(8,128)(2,1)S(1)}, u32[]{:S(2)}, u32[]{:S(2)}) collective-permute-start(bf16[256,256]{1,0:T(8,128)(2,1)S(1)} %get-tuple-element.32), channel_id=1, source_target_pairs={{0,16},{8,24},{16,0},{24,8},{1,17},{9,25},{17,1},{25,9},{2,18},{10... | collective-permute-start | bytes 393224 | tf_op jit(solution)/shard_map/ppermute | solution.py:463
  607.1 8.9 %collective-permute-start.18 = (bf16[256,256]{1,0:T(8,128)(2,1)S(1)}, bf16[256,256]{1,0:T(8,128)(2,1)S(1)}, u32[]{:S(2)}, u32[]{:S(2)}) collective-permute-start(bf16[256,256]{1,0:T(8,128)(2,1)S(1)} %get-tuple-element.31), channel_id=1, source_target_pairs={{0,24},{8,0},{16,8},{24,16},{1,25},{9,1},{17,9},{25,17},{2,26},{10... | collective-permute-start | bytes 393224 | tf_op jit(solution)/shard_map/ppermute | solution.py:463
  611.2 4.7 copy-start.21
  616.0 0.6 copy-start.22
  616.0 0.7 copy-start.23
Sparse Core Ops, SparseCore 0:
  45.0 63.0 all-gather.3
  143.1 78.2 reduce-scatter.5
  283.6 76.2 reduce-scatter.7
  375.5 80.2 all-gather.7
  457.2 79.2 all-gather.5
  559.5 39.2 reduce-scatter.9
